TPU v7x, 256 devices: a whole 4x4x8 slice. The times are simulated.
256 devices in a mesh: section: 4 (over x), dp: 8 (over z_hi, core), tp: 8 (over z_lo, y).
Axes of the slice: x: 4, y: 4, z: 8 (z_hi: 4, z_lo: 2; z = z_hi * 2 + z_lo), core: 2. Of those that a mesh axis runs over, the one named last changes fastest.
Arguments:
- rollout_rows: bfloat16 [1536, 4096], P(('section', 'tp'), 'dp'), may hold values from -6 to 6
- segment_ids: int32 [1536], P(('section', 'tp')), may hold values from 0 to 11, never falling along the last dimension, each value on 1 to 768 neighbouring positions
- gate_weights: bfloat16 [4, 4096, 14336], P('section', 'dp', 'tp'), may hold values from -0.09375 to 0.09375
- up_weights: bfloat16 [4, 4096, 14336], P('section', 'dp', 'tp'), may hold values from -0.09375 to 0.09375
- down_weights: bfloat16 [4, 14336, 4096], P('section', 'tp', 'dp'), may hold values from -0.046875 to 0.046875
- head_weights: bfloat16 [4, 4096], P('section', 'dp'), may hold values from -0.09375 to 0.09375
Outputs:
- advantages: float32 [1536], P(('section', 'tp'))
- returns: float32 [1536], P(('section', 'tp'))
Inputs may be any that keep to these rules, and one draw needn't show every extreme that they name: `segment_ids`: ids never fall along the pack; each response holds 1 to 768 consecutive rows, one exactly 768; all 12 responses occur.
All inputs are finite; a program needn't handle non-finite values.
Results may differ from a plain program's by a relative error of at most 0.00076.
Values may be sent and summed in bfloat16 or wider, within the bound.
No kernel may reach another device: no remote copies, remote signals or barrier semaphores. Data moves between devices by JAX's collectives and lax.ppermute only.
A program may use at most 128 MiB of HBM per device.

v0:
```python
import jax
import jax.numpy as jnp
from jax import lax
from jax.sharding import PartitionSpec as P

epsilon = 1e-05
kl_coef = 0.2
discount = 1.0
trace_decay = 1.0


def from_behind(block, axis, distance):
    devices = range(lax.axis_size(axis))
    route = [(i - distance, i) for i in devices if i - distance in devices]
    return lax.ppermute(block, axis, route)


def entering(shard, axis, combine, identity):
    devices, here = (lax.axis_size(axis), lax.axis_index(axis))
    everything = jax.tree.map(lambda part: lax.all_gather(part, axis), shard)
    start = jax.tree.map(
        lambda part, zero: jnp.broadcast_to(jnp.asarray(zero, part.dtype), part.shape),
        shard,
        identity,
    )

    def lap(k, before):
        at = devices - 1 - k
        reached = at > here
        new = combine(before, jax.tree.map(lambda part: part[at], everything))
        return jax.tree.map(lambda a, b: jnp.where(reached, a, b), new, before)

    return lax.fori_loop(0, devices, lap, start)


def shards(rollout_rows, segment_ids, gate_weights, up_weights, down_weights, head_weights):
    sections = lax.axis_size("section")
    tensor_ways = lax.axis_size("tp")
    owners = lax.axis_size("dp")
    block_rows = rollout_rows.shape[0]
    width_part = rollout_rows.shape[1]
    arrived = lax.all_gather(rollout_rows, ("section", "tp"), axis=0, tiled=True)
    ordered = (
        arrived.reshape(sections, tensor_ways, block_rows, width_part)
        .transpose(1, 0, 2, 3)
        .reshape(-1, width_part)
    )
    gate_part = gate_weights[0]
    up_part = up_weights[0]
    units = gate_part.shape[1]
    summed = lax.psum_scatter(
        jnp.concatenate(
            (
                jnp.dot(ordered, gate_part, preferred_element_type=jnp.float32),
                jnp.dot(ordered, up_part, preferred_element_type=jnp.float32),
            ),
            axis=1,
        ),
        "dp",
        scatter_dimension=0,
        tiled=True,
    )
    gate_sum = summed[:, :units]
    up_sum = summed[:, units:]
    hidden = (jax.nn.silu(gate_sum) * up_sum).astype(jnp.bfloat16)
    down_part = down_weights[0]
    projected = jnp.dot(
        lax.all_gather(hidden, "dp", axis=0, tiled=True),
        down_part,
        preferred_element_type=jnp.float32,
    )
    mixed = lax.psum_scatter(projected, "tp", scatter_dimension=0, tiled=True)
    own_rows = mixed.shape[0]
    residual = lax.dynamic_slice_in_dim(ordered, lax.axis_index("tp") * own_rows, own_rows, 0)
    stream = residual.astype(jnp.float32) + mixed
    head_part = head_weights[0].astype(jnp.float32)
    squares, along = lax.psum(
        (jnp.sum(stream * stream, axis=1), jnp.sum(stream * head_part, axis=1)), "dp"
    )
    scores = along / jnp.sqrt(squares / (width_part * owners) + epsilon)
    joined = lax.all_to_all(
        scores.reshape(sections, block_rows), "section", split_axis=0, concat_axis=0, tiled=True
    )
    policy_score = joined[0]
    ref_score = joined[1]
    reward_score = joined[2]
    values = joined[3]
    segments = segment_ids.astype(jnp.float32)
    next_value, next_segment = from_behind((values[:1], segments[:1]), ("section", "tp"), -1)
    later_values = jnp.concatenate((values[1:], next_value))
    later_segments = jnp.concatenate((segments[1:], next_segment))
    same = (later_segments == segments).astype(jnp.float32)
    rewards = -kl_coef * (policy_score - ref_score) + (1.0 - same) * reward_score
    deltas = rewards + discount * later_values * same - values
    factors = discount * trace_decay * same

    def advance(carried, inputs):
        delta_now, factor_now = inputs
        updated = delta_now + factor_now * carried
        return (updated, updated)

    final_state, local_advantage = lax.scan(
        advance, jnp.float32(0.0), (deltas, factors), reverse=True
    )
    products = jnp.cumprod(factors[::-1])[::-1]

    def compose(earlier, later):
        return (later[0] + later[1] * earlier[0], later[1] * earlier[1])

    incoming, through = entering(
        (local_advantage[0], products[0]),
        ("section", "tp"),
        compose,
        (jnp.float32(0.0), jnp.float32(1.0)),
    )
    advantages = local_advantage + products * incoming
    return (advantages, advantages + values)


def solution(mesh):
    return jax.shard_map(
        shards,
        mesh=mesh,
        in_specs=(
            P(("section", "tp"), "dp"),
            P(("section", "tp")),
            P("section", "dp", "tp"),
            P("section", "dp", "tp"),
            P("section", "tp", "dp"),
            P("section", "dp"),
        ),
        out_specs=(P(("section", "tp")), P(("section", "tp"))),
        check_vma=False,
    )
```

profile of v0, /device:TPU:8, one launch (start us, length us, event | category | flops | bytes accessed | tf_op | source)
XLA Modules:
  0.0 848.5 jit_solution(421732016931791345)
XLA Ops:
  7.2 0.7 all-gather.4.cloned.1.call-update
  8.0 159.3 %all-gather.4.cloned.1.call-done = bf16[1536,512]{1,0:T(8,128)(2,1)} async-done(((bf16[48,512]{1,0:T(8,128)(2,1)}), bf16[1536,512]{1,0:T(8,128)(2,1)}) %all-gather.4.cloned.1.call-update) | async-done | bytes 1572880 | tf_op jit(solution)/shard_map/all_gather | solution.py:42
  167.2 1.5 copy.10
  168.8 3.0 fusion.2
  171.8 3.0 fusion.4
  174.9 8.0 pad_maximum_fusion
  183.0 225.0 %reduce-scatter.3.cloned.1.call-done = f32[192,3584]{1,0:T(8,128)} async-done(((f32[1536,3584]{1,0:T(8,128)}), f32[192,3584]{1,0:T(8,128)}) %reduce-scatter.3.cloned.1.call-update) | async-done | bytes 2752528 | tf_op jit(solution)/shard_map/reduce_scatter | solution.py:51
  408.0 3.0 fusion.6
  411.1 63.9 %all-gather.6.cloned.1.call-done = bf16[1536,1792]{1,0:T(8,128)(2,1)} async-done(((bf16[192,1792]{1,0:T(8,128)(2,1)}), bf16[1536,1792]{1,0:T(8,128)(2,1)}) %all-gather.6.cloned.1.call-update) | async-done | bytes 5505040 | tf_op jit(solution)/shard_map/all_gather | solution.py:68
  475.0 7.8 fusion
  482.9 0.6 copy-done.2
  483.5 2.8 collective-permute-start
  486.4 0.7 dynamic-slice
  487.1 1.9 collective-permute-done
  489.0 0.6 fusion.11
  489.8 42.0 %reduce-scatter.5.cloned.1.call-done = f32[192,512]{1,0:T(8,128)} async-done(((f32[1536,512]{1,0:T(8,128)}), f32[192,512]{1,0:T(8,128)}) %reduce-scatter.5.cloned.1.call-update) | async-done | bytes 393232 | tf_op jit(solution)/shard_map/reduce_scatter | solution.py:72
  531.8 1.2 multiply_reduce_fusion
  532.9 14.2 %all-reduce.3 = (f32[192]{0:T(256)S(1)}, f32[192]{0:T(256)S(1)}) all-reduce(f32[192]{0:T(256)S(1)} %get-tuple-element.240, f32[192]{0:T(256)S(1)} %get-tuple-element.239), channel_id=1, replica_groups=mesh['section'=4,'dp'=8,'tp'=8] {'dp'}, use_global_device_ids=true, to_apply=%region_3.4 | all-reduce | flops 384 | bytes 3072 | tf_op jit(solution)/shard_map/psum | solution.py:77
  547.2 0.7 all_to_all.6
  547.8 4.1 all-to-all-start
  552.8 1.3 bitcast_dynamic-update-slice_fusion
  554.1 3.1 all-to-all-done
  557.3 3.9 collective-permute-start.1
  561.2 1.7 collective-permute-done.1
  562.8 0.7 bitcast_subtract_fusion
  563.5 118.4 %while.31 = (s32[]{:T(128)}, f32[]{:T(128)}, f32[48]{0:T(128)S(1)}, f32[48]{0:T(128)S(1)}, f32[48]{0:T(128)S(1)}, /*index=5*/s32[]{:T(128)}, s32[]{:T(128)}) while((s32[]{:T(128)}, f32[]{:T(128)}, f32[48]{0:T(128)S(1)}, f32[48]{0:T(128)S(1)}, f32[48]{0:T(128)S(1)}, /*index=5*/s32[]{:T(128)}, s32[]{:T(128)}) %tuple.72), condition=%wide.region_7.8_spmd, body=%wide.region_6.7_spmd.sunk | while | flops 5 | bytes 157 | solution.py:102
  563.5 0.6 dynamic_slice.49
  566.0 0.6 dynamic_slice.49
  568.5 0.6 dynamic_slice.49
  570.9 0.6 dynamic_slice.49
  573.4 0.6 dynamic_slice.49
  575.9 0.6 dynamic_slice.49
  578.3 0.6 dynamic_slice.49
  580.8 0.6 dynamic_slice.49
  583.3 0.6 dynamic_slice.49
  585.7 0.6 dynamic_slice.49
  588.2 0.6 dynamic_slice.49
  590.7 0.6 dynamic_slice.49
  593.1 0.6 dynamic_slice.49
  595.6 0.6 dynamic_slice.49
  598.0 0.6 dynamic_slice.49
  600.5 0.6 dynamic_slice.49
  605.4 0.6 dynamic_slice.49
  607.9 0.6 dynamic_slice.49
  610.4 0.6 dynamic_slice.49
  681.9 0.8 slice_dynamic-update-slice_fusion
  682.7 78.8 %all-reduce.2 = (f32[32]{0:T(128)S(1)}, f32[32]{0:T(128)S(1)}) all-reduce(f32[32]{0:T(128)S(1)} %slice_dynamic-update-slice_fusion, f32[32]{0:T(128)S(1)} %bitcast_dynamic-update-slice_fusion), channel_id=1, replica_groups=mesh['section'=4,'dp'=8,'tp'=8] {'section','tp'}, use_global_device_ids=true, to_apply=%add | all-reduce | flops 64 | bytes 512
  761.4 80.0 %while.32 = (s32[]{:T(128)}, f32[]{:T(128)}, s32[]{:T(128)}, f32[32]{0:T(128)S(1)}, f32[32]{0:T(128)S(1)}, /*index=5*/s32[]{:T(128)}, s32[]{:T(128)}, s32[]{:T(128)}, s32[]{:T(128)}) while((s32[]{:T(128)}, f32[]{:T(128)}, s32[]{:T(128)}, f32[32]{0:T(128)S(1)}, f32[32]{0:T(128)S(1)}, /*index=5*/s32[]{:T(128)}, s32[]{:T(128)}, s32[]{:T(128)}, ...), condition=%wide.region_10.11_spmd, body=%wide.region_9.10_spmd.sunk | while | flops 10 | bytes 217 | solution.py:33
  (221 shorter events, 89.6 us)
Async XLA Ops:
  7.2 161.6 %copy-start = (bf16[1,512,1792]{2,1,0:T(8,128)(2,1)S(1)}, bf16[1,512,1792]{2,1,0:T(8,128)(2,1)}, u32[]{:S(2)}) copy-start(bf16[1,512,1792]{2,1,0:T(8,128)(2,1)} %param.13) | copy-start | bytes 5505028
  7.2 160.1 %all-gather.4.cloned.1.call-start = ((), (), s32[]{:S(2)}) async-start(), calls=%async_computation.3 | async-start | bytes 1622016 | tf_op jit(solution)/shard_map/all_gather | solution.py:42
  7.9 400.1 %reduce-scatter.3.cloned.1.call-start = ((), (), s32[]{:S(2)}) async-start(), calls=%async_computation.4 | async-start | bytes 24772608 | tf_op jit(solution)/shard_map/reduce_scatter | solution.py:51
  168.8 3.0 copy-start.3
  182.9 292.1 %all-gather.6.cloned.1.call-start = ((), (), s32[]{:S(2)}) async-start(), calls=%async_computation.5 | async-start | bytes 6193152 | tf_op jit(solution)/shard_map/all_gather | solution.py:68
  411.1 120.7 %reduce-scatter.5.cloned.1.call-start = ((), (), s32[]{:S(2)}) async-start(), calls=%async_computation.6 | async-start | bytes 3538944 | tf_op jit(solution)/shard_map/reduce_scatter | solution.py:72
  482.8 0.7 copy-start.2
  482.8 3.6 copy-start.1
  482.8 3.6 copy-start.4
  483.5 5.5 collective-permute-start
  547.8 9.4 %all-to-all-start = ((f32[4,1,48]{2,1,0:T(1,128)}), f32[4,1,48]{2,1,0:T(1,128)S(1)}, u32[]{:S(2)}, u32[]{:S(2)}) async-start(f32[4,1,48]{2,1,0:T(1,128)} %all_to_all.6), calls=%async_computation.2 | async-start | bytes 4096 | tf_op jit(solution)/shard_map/all_to_all | solution.py:81
  557.3 5.5 collective-permute-start.1
Sparse Core Ops, SparseCore 0:
  9.8 157.3 all-gather.3
  183.1 224.9 reduce-scatter.2
  411.2 63.8 all-gather.5
  483.0 48.7 reduce-scatter.4
where the time goes:
time: 850 us; the launch traced here: 848 us
  waiting for transfers between devices  498 us (59%)
  local copies, waits for them, and re-layouts  105 us (12%)
  loops' own time  99.4 us (12%)
  blocking collectives  93 us (11%)
  other arithmetic  14.3 us (2%)
  matrix products  13.9 us (2%)
  between operations  13.9 us (2%)
  starting transfers between devices  11 us (1%)
    reduce_scatter x1, waiting for transfers between devices, shards(): lax.psum_scatter(jnp.concatenate((jnp.dot(ordered, gate_part, preferred_e...  225 us
    all_gather x1, waiting for transfers between devices, shards(): lax.all_gather(rollout_rows, ('section', 'tp'), axis=0, tiled=True)  159 us
    unnamed x1, blocking collectives  78.8 us
    all_gather x1, waiting for transfers between devices, shards(): lax.all_gather(hidden, 'dp', axis=0, tiled=True)  63.9 us
    another operation x1, loops' own time, shards(): lax.scan(advance, jnp.float32(0.0), (deltas, factors), reverse=True)  56.9 us
    dynamic_slice x96, local copies, waits for them, and re-layouts, shards(): lax.scan(advance, jnp.float32(0.0), (deltas, factors), reverse=True)  56 us
    another operation x1, loops' own time, entering(): return lax.fori_loop(0, devices, lap, start)  42.6 us
    reduce_scatter x1, waiting for transfers between devices, shards(): mixed = lax.psum_scatter(projected, 'tp', scatter_dimension=0, tiled=True)  42 us
  transfers between devices with their start and end apart: 7, of which 7 were waited for; matrix products, arithmetic and copies ran while one was open for 0% of the time, Pallas kernels for 0%

commit v1 on v0

v1 whole, which is shorter than its diff:
```python
import functools
import jax
import jax.numpy as jnp
from jax import lax
from jax.experimental import pallas as pl
from jax.experimental.pallas import tpu as pltpu
from jax.sharding import Mesh, PartitionSpec as P

EPSILON = 1e-05
KL_COEF = 0.2
AXES = ("section", "zhi", "core", "zlo", "y")
F32, BF16 = jnp.float32, jnp.bfloat16


def spread(block, axes):
    members = lax.axis_size(axes)
    copies = jnp.broadcast_to(block[None], (members,) + block.shape)
    return lax.all_to_all(copies, axes, split_axis=0, concat_axis=0, tiled=True)


def swap(block, axis="core"):
    return lax.ppermute(block, axis, [(0, 1), (1, 0)])


def shift(block, axis, by):
    n = lax.axis_size(axis)
    return lax.ppermute(block, axis, [(i, (i + by) % n) for i in range(n)])


NT = (((1,), (1,)), ((), ()))


def hidden_kernel(core_ref, xa_ref, xa2_ref, xb_ref, xb2_ref, gate_ref, up_ref, out_ref):
    core = core_ref[0]
    units = gate_ref.shape[2]
    rows = out_ref.shape[1]
    gate = jnp.zeros((units, rows), F32)
    up = jnp.zeros((units, rows), F32)
    for z in range(4):
        first = z < 2
        for other in range(2):
            if first:
                part = (xa2_ref if other else xa_ref)[:, 0, z]
            else:
                part = (xb2_ref if other else xb_ref)[0, :, z - 2]
            part = part.reshape(rows, part.shape[-1])
            parity = (1 - core) if other else core
            gate += lax.dot_general(gate_ref[z, parity], part, NT, preferred_element_type=F32)
            up += lax.dot_general(up_ref[z, parity], part, NT, preferred_element_type=F32)
    hidden = gate / (1.0 + jnp.exp(-gate)) * up
    out_ref[...] = hidden.astype(BF16)


def hidden_units(core, xa, xa2, xb, xb2, gate, up):
    units = gate.shape[2]
    rows = xa.shape[0] * xa.shape[3] * xa.shape[4]
    tiles = xa.shape[1]
    a_block = pl.BlockSpec((xa.shape[0], 1) + xa.shape[2:], lambda i, c: (0, i, 0, 0, 0, 0))
    b_block = pl.BlockSpec((1,) + xb.shape[1:], lambda i, c: (i, 0, 0, 0, 0, 0))
    weight = pl.BlockSpec(gate.shape, lambda i, c: (0, 0, 0, 0))
    return pl.pallas_call(
        hidden_kernel,
        grid_spec=pltpu.PrefetchScalarGridSpec(
            num_scalar_prefetch=1,
            grid=(tiles,),
            in_specs=[a_block, a_block, b_block, b_block, weight, weight],
            out_specs=pl.BlockSpec((units, rows), lambda i, c: (0, i)),
        ),
        out_shape=jax.ShapeDtypeStruct((units, rows * tiles), BF16),
        compiler_params=pltpu.CompilerParams(vmem_limit_bytes=48 << 20),
        name="hidden_units",
    )(core, xa, xa2, xb, xb2, gate, up)


def down_kernel(h_ref, down_ref, head_ref, out_ref):
    half = head_ref.shape[0] // 2
    for part in range(2):
        span = slice(part * half, (part + 1) * half)
        product = jnp.dot(down_ref[span, :], h_ref[...], preferred_element_type=F32)
        out_ref[part, 0, :half, :] = product.astype(BF16)
        along = jnp.sum(product * head_ref[span, :], axis=0, keepdims=True)
        high = along.astype(BF16).astype(F32)
        rest = along - high
        middle = rest.astype(BF16).astype(F32)
        low = rest - middle
        pad = jnp.zeros((13, along.shape[1]), F32)
        out_ref[part, 0, half:, :] = jnp.concatenate((high, middle, low, pad), axis=0).astype(BF16)


def down_product(hidden, down, head):
    units, total = hidden.shape
    tiles = 4
    rows = total // tiles
    width = down.shape[0]
    tall = width // 2 + 16
    return pl.pallas_call(
        down_kernel,
        grid=(tiles,),
        in_specs=[
            pl.BlockSpec((units, rows), lambda i: (0, i)),
            pl.BlockSpec(down.shape, lambda i: (0, 0)),
            pl.BlockSpec(head.shape, lambda i: (0, 0)),
        ],
        out_specs=pl.BlockSpec((2, 1, tall, rows), lambda i: (0, i, 0, 0)),
        out_shape=jax.ShapeDtypeStruct((2, tiles, tall, rows), BF16),
        compiler_params=pltpu.CompilerParams(vmem_limit_bytes=48 << 20),
        name="down_product",
    )(hidden, down, head)


def sums_kernel(arrived_ref, residual_ref, head_ref, out_ref):
    half = residual_ref.shape[0]
    residual = residual_ref[...].astype(F32)
    stream = residual
    along = jnp.sum(residual * head_ref[...], axis=0, keepdims=True)
    for member in range(arrived_ref.shape[0]):
        stream += arrived_ref[member, :half, :].astype(F32)
        terms = arrived_ref[member, half:, :].astype(F32)
        along += jnp.sum(terms, axis=0, keepdims=True)
    out_ref[0:1, :] = jnp.sum(stream * stream, axis=0, keepdims=True)
    out_ref[1:2, :] = along


def row_sums(arrived, residual, head):
    return pl.pallas_call(
        sums_kernel,
        out_shape=jax.ShapeDtypeStruct((2, residual.shape[1]), F32),
        name="row_sums",
    )(arrived, residual, head)


def shards(rollout_rows, segment_ids, gate_weights, up_weights, down_weights, head_weights):
    section, zhi, core, zlo, y = (lax.axis_index(axis) for axis in AXES)
    block_rows, width_part = rollout_rows.shape
    dp, tp = ("zhi", "core"), ("zlo", "y")
    owners = lax.axis_size(dp)

    gate = lax.all_to_all(gate_weights[0].T, dp, split_axis=0, concat_axis=0, tiled=True)
    up = lax.all_to_all(up_weights[0].T, dp, split_axis=0, concat_axis=0, tiled=True)
    units = gate.shape[0] // owners
    gate = gate.reshape(4, 2, units, width_part)
    up = up.reshape(4, 2, units, width_part)

    column = spread(rollout_rows, ("zhi", "zlo")).reshape(4, 2, block_rows, width_part)
    xa = spread(spread(column[:2], "y"), "section")
    xb = spread(spread(column[2:], "section"), "y")
    xa2, xb2 = swap(xa), swap(xb)
    here = core.reshape(1).astype(jnp.int32)
    hidden = hidden_units(here, xa, xa2, xb, xb2, gate, up)

    after, before = shift(hidden, "zhi", 1), shift(hidden, "zhi", -1)
    cut = units // 2
    far_top = shift(after[:cut], "zhi", 1)
    far_end = shift(before[cut:], "zhi", -1)
    far = jnp.concatenate((far_top, far_end), axis=0)
    mine = jnp.stack((hidden, after, far, before))
    theirs = swap(mine)
    both = jnp.stack((mine, theirs), axis=1)
    gathered = both.reshape(8 * units, -1)

    down = down_weights[0].reshape(4, 2, units, width_part)
    order = (zhi - jnp.arange(4)) % 4
    down = jnp.take(down, order, axis=0)
    down = jnp.where(core == 0, down, down[:, ::-1])
    down = down.reshape(8 * units, width_part).T
    head = head_weights[0].astype(F32)
    parts = down_product(gathered, down, head.reshape(width_part, 1))
    arrived = lax.all_to_all(
        parts.reshape((8,) + parts.shape[2:]), tp, split_axis=0, concat_axis=0, tiled=True
    )

    half = width_part // 2
    own_a = lax.dynamic_index_in_dim(xa, y, 1, keepdims=False)
    own_b = lax.dynamic_index_in_dim(xb, y, 0, keepdims=False)
    own = jnp.concatenate((own_a, own_b), axis=1)
    own = lax.dynamic_index_in_dim(own, zhi, 1, keepdims=False).reshape(-1, width_part)
    residual = lax.dynamic_slice_in_dim(own, zlo * half, half, 1).T
    own_head = lax.dynamic_slice_in_dim(head, zlo * half, half, 0).reshape(half, 1)
    sums = row_sums(arrived, residual, own_head)
    sums = sums + swap(sums)
    sums = sums + swap(sums, "zlo")
    sums = jnp.sum(spread(sums, "zhi"), axis=0)
    scores = sums[1] / jnp.sqrt(sums[0] / (width_part * owners) + EPSILON)

    everyone = spread(scores, ("section", "y")).reshape(4, -1)
    policy_score, ref_score, reward_score, values = everyone
    segments = spread(segment_ids, ("section", "zlo", "y"))
    flat = segments.reshape(-1)
    same_flat = jnp.concatenate((flat[1:] == flat[:-1], jnp.zeros((1,), bool)))

    def ordered(array):
        array = array.reshape(4, 2, 4, block_rows)
        return array.transpose(2, 0, 1, 3).reshape(-1)

    last = ordered(1.0 - same_flat.astype(F32))
    columns = ordered(flat)
    position = ordered(jnp.arange(flat.shape[0], dtype=jnp.int32))
    own_position = ((section * 2 + zlo) * 4 + y) * block_rows + jnp.arange(block_rows)
    reach = (segment_ids[:, None] == columns[None, :]) & (position[None, :] >= own_position[:, None])
    rewards = -KL_COEF * (policy_score - ref_score) + last * reward_score
    returns = jnp.sum(jnp.where(reach, rewards[None, :], 0.0), axis=1)
    own_values = lax.dynamic_index_in_dim(values.reshape(4, 4, 2, block_rows), y, 0, keepdims=False)
    own_values = lax.dynamic_index_in_dim(own_values, section, 0, keepdims=False)
    own_values = lax.dynamic_index_in_dim(own_values, zlo, 0, keepdims=False)
    return (returns - own_values, returns)


def solution(mesh):
    fine = Mesh(mesh.devices.reshape(4, 4, 2, 2, 4), AXES)
    dp, rows = ("zhi", "core"), ("section", "zlo", "y")
    tp = ("zlo", "y")
    return jax.shard_map(
        shards,
        mesh=fine,
        in_specs=(P(rows, dp), P(rows), P("section", dp, tp), P("section", dp, tp), P("section", tp, dp), P("section", dp)),
        out_specs=(P(rows), P(rows)),
        check_vma=False,
    )
```

time: 850 us -> 378 us (0.44)
  waiting for transfers between devices: 498 us -> 134 us
  loops' own time: 99.4 us -> 0 us
  local copies, waits for them, and re-layouts: 105 us -> 30 us
  starting transfers between devices: 11 us -> 51.9 us
  blocking collectives: 93 us -> 127 us
  Pallas kernels: 0 us -> 21 us
  matrix products: 13.9 us -> 0 us
  between operations: 13.9 us -> 0.92 us
    reduce_scatter x2 -> x0, waiting for transfers between devices: 267 us -> none  [the longest x1 225 us: shards(): lax.psum_scatter(jnp.concatenate((jnp.dot(ordered, gate_part, preferred_e...]
    all_gather x2 -> x0, waiting for transfers between devices: 223 us -> none  [the longest x1 159 us: shards(): lax.all_gather(rollout_rows, ('section', 'tp'), axis=0, tiled=True)]
    all_to_all x0 -> x4, blocking collectives: none -> 127 us  [the longest x3 78.2 us: spread(): return lax.all_to_all(copies, axes, split_axis=0, concat_axis=0, tiled=True)]
    all_to_all x1 -> x7, waiting for transfers between devices: 3.08 us -> 103 us  [the longest x5 51.8 us: spread(): return lax.all_to_all(copies, axes, split_axis=0, concat_axis=0, tiled=True)]
    another operation x2 -> x0, loops' own time: 99.4 us -> none  [the longest x1 56.9 us: shards(): lax.scan(advance, jnp.float32(0.0), (deltas, factors), reverse=True)]
    dynamic_slice x160 -> x1, local copies, waits for them, and re-layouts: 93.4 us -> 0.7 us  [shards(): residual = lax.dynamic_slice_in_dim(own, zlo * half, half, 1).T]
    unnamed x1 -> x0, blocking collectives: 78.8 us -> none
    all_to_all x1 -> x7, starting transfers between devices: 4.13 us -> 40.2 us  [the longest x5 27.2 us: spread(): return lax.all_to_all(copies, axes, split_axis=0, concat_axis=0, tiled=True)]
  transfers between devices with their start and end apart: 7 -> 16, of which waited for: 7 -> 12; matrix products, arithmetic and copies ran while one was open for 0% -> 6% of each run, Pallas kernels for 0% -> 1%
where the time goes in v1:
time: 378 us; the launch traced here: 377 us
  waiting for transfers between devices  134 us (35%)
  blocking collectives  127 us (34%)
  starting transfers between devices  51.9 us (14%)
  local copies, waits for them, and re-layouts  30 us (8%)
  Pallas kernels  21 us (6%)
  other arithmetic  11.8 us (3%)
    all_to_all x3, blocking collectives, spread(): return lax.all_to_all(copies, axes, split_axis=0, concat_axis=0, tiled=True)  78.2 us
    all_to_all x5, waiting for transfers between devices, spread(): return lax.all_to_all(copies, axes, split_axis=0, concat_axis=0, tiled=True)  51.8 us
    all_to_all x1, blocking collectives, shards(): lax.all_to_all(up_weights[0].T, dp, split_axis=0, concat_axis=0, tiled=True)  49.1 us
    all_to_all x1, waiting for transfers between devices, shards(): lax.all_to_all(gate_weights[0].T, dp, split_axis=0, concat_axis=0, tiled=...  36 us
    ppermute x4, waiting for transfers between devices, shift(): return lax.ppermute(block, axis, [(i, (i + by) % n) for i in range(n)])  29.1 us
    all_to_all x5, starting transfers between devices, spread(): return lax.all_to_all(copies, axes, split_axis=0, concat_axis=0, tiled=True)  27.2 us
    all_to_all x1, waiting for transfers between devices, shards(): lax.all_to_all(parts.reshape((8,) + parts.shape[2:]), tp, split_axis=0, c...  15.4 us
    pallas_call x1, Pallas kernels, hidden_units(): pl.pallas_call(hidden_kernel, grid_spec=pltpu.PrefetchScalarGridSpec(num_...  11.4 us
  transfers between devices with their start and end apart: 16, of which 12 were waited for; matrix products, arithmetic and copies ran while one was open for 6% of the time, Pallas kernels for 1%

profile of v1, /device:TPU:8, one launch (start us, length us, event | category | flops | bytes accessed | tf_op | source)
XLA Modules:
  0.0 376.6 jit_solution(2964617476117017730)
XLA Ops:
  0.6 1.0 broadcast_in_dim.39
  1.6 22.9 %all_to_all.65 = bf16[8,48,512]{2,1,0:T(8,128)(2,1)S(1)} all-to-all(bf16[8,48,512]{2,1,0:T(8,128)(2,1)S(1)} %broadcast_in_dim.39), channel_id=1, replica_groups=mesh['section'=4,'zhi'=4,'core'=2,'zlo'=2,'y'=4] {'zhi','zlo'}, dimensions={0} | all-to-all | bytes 786432 | tf_op jit(solution)/shard_map/all_to_all | solution.py:18
  24.7 14.1 %all_to_all.66 = bf16[4,2,2,48,512]{4,3,2,1,0:T(8,128)(2,1)S(1)} all-to-all(bf16[4,2,2,48,512]{4,3,2,1,0:T(8,128)(2,1)S(1)} %broadcast_in_dim.41), channel_id=1, replica_groups=mesh['section'=4,'zhi'=4,'core'=2,'zlo'=2,'y'=4] {'y'}, dimensions={0} | all-to-all | bytes 1572864 | tf_op jit(solution)/shard_map/all_to_all | solution.py:18
  38.8 1.0 broadcast_in_dim.44
  39.7 4.3 %all-to-all-start.4 = ((bf16[4,2,2,48,512]{4,3,2,1,0:T(8,128)(2,1)}), bf16[4,2,2,48,512]{4,3,2,1,0:T(8,128)(2,1)S(1)}, u32[]{:S(2)}, u32[]{:S(2)}) async-start(bf16[4,2,2,48,512]{4,3,2,1,0:T(8,128)(2,1)} %broadcast_in_dim.44), calls=%async_computation.4 | async-start | bytes 1572864 | tf_op jit(solution)/shard_map/all_to_all | solution.py:18
  44.0 3.8 %copy.47 = bf16[1,512,1792]{1,2,0:T(8,128)(2,1)} copy(bf16[1,512,1792]{2,1,0:T(8,128)(2,1)} %param.9) | data formatting | bytes 3670016 | tf_op args[3]
  47.9 5.8 %all-to-all-done.4 = bf16[4,2,2,48,512]{4,3,2,1,0:T(8,128)(2,1)S(1)} async-done(((bf16[4,2,2,48,512]{4,3,2,1,0:T(8,128)(2,1)}), bf16[4,2,2,48,512]{4,3,2,1,0:T(8,128)(2,1)S(1)}, u32[]{:S(2)}, u32[]{:S(2)}) %all-to-all-start.4) | async-done | bytes 786464 | tf_op jit(solution)/shard_map/all_to_all | solution.py:18
  53.7 49.1 %all_to_all.67 = bf16[8,224,512]{2,1,0:T(8,128)(2,1)} all-to-all(bf16[8,224,512]{2,1,0:T(8,128)(2,1)} %bitcast.54), channel_id=1, replica_groups=mesh['section'=4,'zhi'=4,'core'=2,'zlo'=2,'y'=4] {'zhi','core'}, dimensions={0} | all-to-all | bytes 3670016 | tf_op jit(solution)/shard_map/all_to_all | solution.py:139
  103.2 41.1 %all_to_all.68.xa_ref = bf16[4,4,2,2,48,512]{5,4,3,2,1,0:T(8,128)(2,1)} all-to-all(bf16[4,4,2,2,48,512]{5,4,3,2,1,0:T(8,128)(2,1)S(1)} %broadcast_in_dim.42), channel_id=1, replica_groups=mesh['section'=4,'zhi'=4,'core'=2,'zlo'=2,'y'=4] {'section'}, dimensions={0} | all-to-all | bytes 6291456 | tf_op jit(solution)/shard_map/all_to_all | solution.py:18
  144.3 2.2 broadcast_in_dim.84
  146.4 6.1 %all-to-all-start.5 = ((bf16[4,4,2,2,48,512]{5,4,3,2,1,0:T(8,128)(2,1)}), bf16[4,4,2,2,48,512]{5,4,3,2,1,0:T(8,128)(2,1)}, u32[]{:S(2)}, u32[]{:S(2)}) async-start(bf16[4,4,2,2,48,512]{5,4,3,2,1,0:T(8,128)(2,1)} %broadcast_in_dim.84), calls=%async_computation.5 | async-start | bytes 6291456 | tf_op jit(solution)/shard_map/all_to_all | solution.py:18
  152.5 3.9 %copy.46 = bf16[1,512,1792]{1,2,0:T(8,128)(2,1)} copy(bf16[1,512,1792]{2,1,0:T(8,128)(2,1)} %param.8) | data formatting | bytes 3670016 | tf_op args[2]
  156.4 31.4 %all-to-all-done.5.xb_ref = bf16[4,4,2,2,48,512]{5,4,3,2,1,0:T(8,128)(2,1)} async-done(((bf16[4,4,2,2,48,512]{5,4,3,2,1,0:T(8,128)(2,1)}), bf16[4,4,2,2,48,512]{5,4,3,2,1,0:T(8,128)(2,1)}, u32[]{:S(2)}, u32[]{:S(2)}) %all-to-all-start.5) | async-done | bytes 3145760 | tf_op jit(solution)/shard_map/all_to_all | solution.py:18
  187.8 4.3 %all-to-all-start.6 = ((bf16[8,224,512]{2,1,0:T(8,128)(2,1)}), bf16[8,224,512]{2,1,0:T(8,128)(2,1)}, u32[]{:S(2)}, u32[]{:S(2)}) async-start(bf16[8,224,512]{2,1,0:T(8,128)(2,1)} %bitcast.53), calls=%async_computation.6 | async-start | bytes 3670016 | tf_op jit(solution)/shard_map/all_to_all | solution.py:138
  192.7 36.0 %all-to-all-done.6 = bf16[8,224,512]{2,1,0:T(8,128)(2,1)} async-done(((bf16[8,224,512]{2,1,0:T(8,128)(2,1)}), bf16[8,224,512]{2,1,0:T(8,128)(2,1)}, u32[]{:S(2)}, u32[]{:S(2)}) %all-to-all-start.6) | async-done | bytes 1835040 | tf_op jit(solution)/shard_map/all_to_all | solution.py:138
  228.8 1.5 copy-done.2
  230.2 11.4 %hidden_units.1 = bf16[224,1536]{1,0:T(8,128)(2,1)S(1)} custom-call(s32[1]{0:T(128)} %bitcast.2.core_ref, bf16[4,4,2,2,48,512]{5,4,3,2,1,0:T(8,128)(2,1)} %all_to_all.68.xa_ref, bf16[4,4,2,2,48,512]{5,4,3,2,1,0:T(8,128)(2,1)} %collective-permute-done.xa2_ref, bf16[4,4,2,2,48,512]{5,4,3,2,1,0:T(8,128)(2,1)} %all-to-all-done.5.xb_ref, ...), custom_call_target="tpu_custom_call" | custom-call | tf_op jit(solution)/shard_map/hidden_units/pallas_call | solution.py:61
  242.2 3.7 collective-permute-start.4
  245.9 19.0 %collective-permute-done.2 = bf16[224,1536]{1,0:T(8,128)(2,1)S(1)} collective-permute-done((bf16[224,1536]{1,0:T(8,128)(2,1)S(1)}, bf16[224,1536]{1,0:T(8,128)(2,1)S(1)}, u32[]{:S(2)}, u32[]{:S(2)}) %collective-permute-start.2) | collective-permute-done | bytes 688160 | tf_op jit(solution)/shard_map/ppermute | solution.py:27
  264.9 2.6 collective-permute-start.3
  267.4 1.4 collective-permute-done.4
  268.9 2.9 collective-permute-start.5
  271.8 7.5 %collective-permute-done.3 = bf16[112,1536]{1,0:T(8,128)(2,1)S(1)} collective-permute-done((bf16[112,1536]{1,0:T(8,128)(2,1)S(1)}, bf16[112,1536]{1,0:T(8,128)(2,1)S(1)}, u32[]{:S(2)}, u32[]{:S(2)}) %collective-permute-start.3) | collective-permute-done | bytes 344096 | tf_op jit(solution)/shard_map/ppermute | solution.py:27
  279.2 1.2 collective-permute-done.5
  280.5 2.7 fusion.13
  283.3 1.9 gather_fusion
  285.2 1.7 broadcast_select_fusion
  286.9 1.6 reverse_select_fusion
  288.5 2.8 copy.49
  291.5 3.1 pad_maximum_fusion
  294.6 2.8 copy.48
  297.5 7.1 %down_product.1 = bf16[2,4,272,384]{3,2,1,0:T(8,128)(2,1)} custom-call(bf16[1792,1536]{1,0:T(8,128)(2,1)} %bitcast.52, bf16[512,1792]{1,0:T(8,128)(2,1)S(1)} %bitcast.50, f32[512,1]{1,0:T(8,128)S(1)} %copy.50.head_ref), custom_call_target="tpu_custom_call" | custom-call | tf_op jit(solution)/shard_map/down_product/pallas_call | solution.py:96
  304.6 8.7 %all-to-all-start.8 = ((bf16[8,272,384]{2,1,0:T(8,128)(2,1)}), bf16[8,272,384]{2,1,0:T(8,128)(2,1)S(1)}, u32[]{:S(2)}, u32[]{:S(2)}) async-start(bf16[8,272,384]{2,1,0:T(8,128)(2,1)} %bitcast.25), calls=%async_computation.8 | async-start | bytes 3342336 | tf_op jit(solution)/shard_map/all_to_all | solution.py:168
  313.2 0.8 copy.52.head_ref
  314.0 1.2 dynamic-slice_bitcast_fusion
  315.2 1.2 dynamic-slice_bitcast_fusion.1
  316.6 0.7 constant_dynamic-slice_fusion.2
  317.3 1.7 copy.56
  319.1 15.4 %all-to-all-done.8.arrived_ref = bf16[8,272,384]{2,1,0:T(8,128)(2,1)S(1)} async-done(((bf16[8,272,384]{2,1,0:T(8,128)(2,1)}), bf16[8,272,384]{2,1,0:T(8,128)(2,1)S(1)}, u32[]{:S(2)}, u32[]{:S(2)}) %all-to-all-start.8) | async-done | bytes 1671200 | tf_op jit(solution)/shard_map/all_to_all | solution.py:168
  335.2 5.3 %all-to-all-start = ((s32[32,1,48]{2,1,0:T(1,128)}), s32[32,1,48]{2,1,0:T(1,128)S(1)}, u32[]{:S(2)}, u32[]{:S(2)}) async-start(s32[32,1,48]{2,1,0:T(1,128)} %broadcast_in_dim.38), calls=%async_computation | async-start | bytes 32768 | tf_op jit(solution)/shard_map/all_to_all | solution.py:18
  340.4 2.5 row_sums.1
  343.0 1.3 collective-permute-done.7
  345.0 1.5 collective-permute-start.8
  346.5 1.0 all-to-all-done
  349.4 4.6 %all-to-all-start.9 = ((f32[4,2,384]{2,1,0:T(2,128)}), f32[4,2,384]{2,1,0:T(2,128)S(1)}, u32[]{:S(2)}, u32[]{:S(2)}) async-start(f32[4,2,384]{2,1,0:T(2,128)} %broadcast_in_dim.87), calls=%async_computation.9 | async-start | bytes 24576 | tf_op jit(solution)/shard_map/all_to_all | solution.py:18
  354.1 7.7 %all-to-all-done.9 = f32[4,2,384]{2,1,0:T(2,128)S(1)} async-done(((f32[4,2,384]{2,1,0:T(2,128)}), f32[4,2,384]{2,1,0:T(2,128)S(1)}, u32[]{:S(2)}, u32[]{:S(2)}) %all-to-all-start.9) | async-done | bytes 12320 | tf_op jit(solution)/shard_map/all_to_all | solution.py:18
  362.4 7.0 %all-to-all-start.10 = ((f32[16,1,384]{2,1,0:T(1,128)}), f32[16,1,384]{2,1,0:T(1,128)S(1)}, u32[]{:S(2)}, u32[]{:S(2)}) async-start(f32[16,1,384]{2,1,0:T(1,128)} %broadcast_in_dim.88), calls=%async_computation.10 | async-start | bytes 49152 | tf_op jit(solution)/shard_map/all_to_all | solution.py:18
  369.8 5.9 %all-to-all-done.10 = f32[16,1,384]{2,1,0:T(1,128)S(1)} async-done(((f32[16,1,384]{2,1,0:T(1,128)}), f32[16,1,384]{2,1,0:T(1,128)S(1)}, u32[]{:S(2)}, u32[]{:S(2)}) %all-to-all-start.10) | async-done | bytes 24608 | tf_op jit(solution)/shard_map/all_to_all | solution.py:18
  (62 shorter events, 7.4 us)
Async XLA Ops:
  0.6 282.6 %copy-start = (bf16[1,1792,512]{2,1,0:T(8,128)(2,1)S(1)}, bf16[1,1792,512]{2,1,0:T(8,128)(2,1)}, u32[]{:S(2)}) copy-start(bf16[1,1792,512]{2,1,0:T(8,128)(2,1)} %param.10) | copy-start | bytes 5505028
  39.7 13.9 %all-to-all-start.4 = ((bf16[4,2,2,48,512]{4,3,2,1,0:T(8,128)(2,1)}), bf16[4,2,2,48,512]{4,3,2,1,0:T(8,128)(2,1)S(1)}, u32[]{:S(2)}, u32[]{:S(2)}) async-start(bf16[4,2,2,48,512]{4,3,2,1,0:T(8,128)(2,1)} %broadcast_in_dim.44), calls=%async_computation.4 | async-start | bytes 1572864 | tf_op jit(solution)/shard_map/all_to_all | solution.py:18
  146.4 41.3 %all-to-all-start.5 = ((bf16[4,4,2,2,48,512]{5,4,3,2,1,0:T(8,128)(2,1)}), bf16[4,4,2,2,48,512]{5,4,3,2,1,0:T(8,128)(2,1)}, u32[]{:S(2)}, u32[]{:S(2)}) async-start(bf16[4,4,2,2,48,512]{5,4,3,2,1,0:T(8,128)(2,1)} %broadcast_in_dim.84), calls=%async_computation.5 | async-start | bytes 6291456 | tf_op jit(solution)/shard_map/all_to_all | solution.py:18
  187.8 41.0 %all-to-all-start.6 = ((bf16[8,224,512]{2,1,0:T(8,128)(2,1)}), bf16[8,224,512]{2,1,0:T(8,128)(2,1)}, u32[]{:S(2)}, u32[]{:S(2)}) async-start(bf16[8,224,512]{2,1,0:T(8,128)(2,1)} %bitcast.53), calls=%async_computation.6 | async-start | bytes 3670016 | tf_op jit(solution)/shard_map/all_to_all | solution.py:138
  192.1 36.6 %collective-permute-start = (bf16[4,4,2,2,48,512]{5,4,3,2,1,0:T(8,128)(2,1)}, bf16[4,4,2,2,48,512]{5,4,3,2,1,0:T(8,128)(2,1)}, u32[]{:S(2)}, u32[]{:S(2)}) collective-permute-start(bf16[4,4,2,2,48,512]{5,4,3,2,1,0:T(8,128)(2,1)} %all_to_all.68.xa_ref), channel_id=1, source_target_pairs={{0,8},{8,0},{1,9},{9,1},{2,10},{10,2},{3,11},{11,3},{4,12},{12,4},... | collective-permute-start | bytes 9437192 | tf_op jit(solution)/shard_map/ppermute | solution.py:22
  192.5 36.3 %collective-permute-start.1 = (bf16[4,4,2,2,48,512]{5,4,3,2,1,0:T(8,128)(2,1)}, bf16[4,4,2,2,48,512]{5,4,3,2,1,0:T(8,128)(2,1)}, u32[]{:S(2)}, u32[]{:S(2)}) collective-permute-start(bf16[4,4,2,2,48,512]{5,4,3,2,1,0:T(8,128)(2,1)} %all-to-all-done.5.xb_ref), channel_id=1, source_target_pairs={{0,8},{8,0},{1,9},{9,1},{2,10},{10,2},{3,11},{11,3},{4,12},{12,4},... | collective-permute-start | bytes 9437192 | tf_op jit(solution)/shard_map/ppermute | solution.py:22
  228.7 1.5 copy-start.2
  241.6 23.2 %collective-permute-start.2 = (bf16[224,1536]{1,0:T(8,128)(2,1)S(1)}, bf16[224,1536]{1,0:T(8,128)(2,1)S(1)}, u32[]{:S(2)}, u32[]{:S(2)}) collective-permute-start(bf16[224,1536]{1,0:T(8,128)(2,1)S(1)} %hidden_units.1), channel_id=1, source_target_pairs={{0,16},{16,32},{32,48},{48,0},{1,17},{17,33},{33,49},{49,1},{2,18}... | collective-permute-start | bytes 2064392 | tf_op jit(solution)/shard_map/ppermute | solution.py:27
  242.2 26.7 %collective-permute-start.4 = (bf16[224,1536]{1,0:T(8,128)(2,1)S(1)}, bf16[224,1536]{1,0:T(8,128)(2,1)S(1)}, u32[]{:S(2)}, u32[]{:S(2)}) collective-permute-start(bf16[224,1536]{1,0:T(8,128)(2,1)S(1)} %hidden_units.1), channel_id=1, source_target_pairs={{0,48},{16,0},{32,16},{48,32},{1,49},{17,1},{33,17},{49,33},{2,50}... | collective-permute-start | bytes 2064392 | tf_op jit(solution)/shard_map/ppermute | solution.py:27
  264.9 14.4 %collective-permute-start.3 = (bf16[112,1536]{1,0:T(8,128)(2,1)S(1)}, bf16[112,1536]{1,0:T(8,128)(2,1)S(1)}, u32[]{:S(2)}, u32[]{:S(2)}) collective-permute-start(bf16[112,1536]{1,0:T(8,128)(2,1)S(1)} %slice.46), channel_id=1, source_target_pairs={{0,16},{16,32},{32,48},{48,0},{1,17},{17,33},{33,49},{49,1},{2,18}... | collective-permute-start | bytes 1032200 | tf_op jit(solution)/shard_map/ppermute | solution.py:27
  268.9 11.6 %collective-permute-start.5 = (bf16[112,1536]{1,0:T(8,128)(2,1)S(1)}, bf16[112,1536]{1,0:T(8,128)(2,1)S(1)}, u32[]{:S(2)}, u32[]{:S(2)}) collective-permute-start(bf16[112,1536]{1,0:T(8,128)(2,1)S(1)} %slice.47), channel_id=1, source_target_pairs={{0,48},{16,0},{32,16},{48,32},{1,49},{17,1},{33,17},{49,33},{2,50}... | collective-permute-start | bytes 1032200 | tf_op jit(solution)/shard_map/ppermute | solution.py:27
  283.2 8.3 %collective-permute-start.6 = (bf16[4,224,1536]{2,1,0:T(8,128)(2,1)}, bf16[4,224,1536]{2,1,0:T(8,128)(2,1)}, u32[]{:S(2)}, u32[]{:S(2)}) collective-permute-start(bf16[4,224,1536]{2,1,0:T(8,128)(2,1)} %get-tuple-element.6), channel_id=1, source_target_pairs={{0,8},{8,0},{1,9},{9,1},{2,10},{10,2},{3,11},{11,3},{4,12},{12,4},... | collective-permute-start | bytes 8257544 | tf_op jit(solution)/shard_map/ppermute | solution.py:22
  288.5 2.8 copy-start.4
  304.6 29.9 %all-to-all-start.8 = ((bf16[8,272,384]{2,1,0:T(8,128)(2,1)}), bf16[8,272,384]{2,1,0:T(8,128)(2,1)S(1)}, u32[]{:S(2)}, u32[]{:S(2)}) async-start(bf16[8,272,384]{2,1,0:T(8,128)(2,1)} %bitcast.25), calls=%async_computation.8 | async-start | bytes 3342336 | tf_op jit(solution)/shard_map/all_to_all | solution.py:168
  315.2 19.3 %copy-start.5 = (s32[48]{0:T(128)S(1)}, s32[48]{0:T(128)}, u32[]{:S(2)}) copy-start(s32[48]{0:T(128)} %param.7) | copy-start | bytes 580
  316.4 60.2 %copy-start.1 = (bf16[1,1792,512]{2,1,0:T(8,128)(2,1)S(1)}, bf16[1,1792,512]{2,1,0:T(8,128)(2,1)}, u32[]{:S(2)}) copy-start(bf16[1,1792,512]{2,1,0:T(8,128)(2,1)} %param.10) | copy-start | bytes 5505028
  334.5 5.9 %copy-start.3 = (bf16[8,272,384]{2,1,0:T(8,128)(2,1)}, bf16[8,272,384]{2,1,0:T(8,128)(2,1)S(1)}, u32[]{:S(2)}) copy-start(bf16[8,272,384]{2,1,0:T(8,128)(2,1)S(1)} %all-to-all-done.8.arrived_ref) | copy-start | bytes 5013508
  335.2 12.4 %all-to-all-start = ((s32[32,1,48]{2,1,0:T(1,128)}), s32[32,1,48]{2,1,0:T(1,128)S(1)}, u32[]{:S(2)}, u32[]{:S(2)}) async-start(s32[32,1,48]{2,1,0:T(1,128)} %broadcast_in_dim.38), calls=%async_computation | async-start | bytes 32768 | tf_op jit(solution)/shard_map/all_to_all | solution.py:18
  342.9 1.4 collective-permute-start.7
  345.0 3.8 %collective-permute-start.8 = (f32[2,384]{1,0:T(2,128)S(1)}, f32[2,384]{1,0:T(2,128)S(1)}, u32[]{:S(2)}, u32[]{:S(2)}) collective-permute-start(f32[2,384]{1,0:T(2,128)S(1)} %add.132), channel_id=1, source_target_pairs={{0,4},{4,0},{1,5},{5,1},{2,6},{6,2},{3,7},{7,3},{8,12},{12,8},{9,1... | collective-permute-start | bytes 9224 | tf_op jit(solution)/shard_map/ppermute | solution.py:22
  349.4 12.3 %all-to-all-start.9 = ((f32[4,2,384]{2,1,0:T(2,128)}), f32[4,2,384]{2,1,0:T(2,128)S(1)}, u32[]{:S(2)}, u32[]{:S(2)}) async-start(f32[4,2,384]{2,1,0:T(2,128)} %broadcast_in_dim.87), calls=%async_computation.9 | async-start | bytes 24576 | tf_op jit(solution)/shard_map/all_to_all | solution.py:18
  362.4 13.2 %all-to-all-start.10 = ((f32[16,1,384]{2,1,0:T(1,128)}), f32[16,1,384]{2,1,0:T(1,128)S(1)}, u32[]{:S(2)}, u32[]{:S(2)}) async-start(f32[16,1,384]{2,1,0:T(1,128)} %broadcast_in_dim.88), calls=%async_computation.10 | async-start | bytes 49152 | tf_op jit(solution)/shard_map/all_to_all | solution.py:18
  376.1 0.5 copy-start.6
